TPU v7x, 256 devices: a whole 4x4x8 slice. The times are simulated.
256 devices in a mesh: row: 2 (over x_lo), col: 128 (over x_hi, y, z, core).
Axes of the slice: x: 4 (x_hi: 2, x_lo: 2; x = x_hi * 2 + x_lo), y: 4, z: 8, core: 2. Of those that a mesh axis runs over, the one named last changes fastest.
Arguments:
- matrix: float32 [64, 2, 128, 1, 128, 128], P(None, 'row', None, None, 'col'), may hold values from -0.25 to 1.5, as said below
Outputs:
- factored: float32 [64, 2, 128, 1, 128, 128], P(None, 'row', None, None, 'col')
Inputs may be any that keep to these rules, and one draw needn't show every extreme that they name: matrix read as A is symmetric and positive definite, its eigenvalues between 0.4 and 8.
All inputs are finite; a program needn't handle non-finite values.
Results may differ from a plain program's by a relative error of at most 0.0001.
Values sent between devices are 32-bit elements; how exact they have to be, the bound alone decides.
A program may use at most 64 MiB of HBM per device.

v0:
```python
import jax
import jax.numpy as jnp
from jax import lax
from jax.sharding import PartitionSpec as P


def from_root(x, axis, root):
    mine = lax.axis_index(axis) == root
    return lax.psum(jnp.where(mine, x, jnp.zeros_like(x)), axis)


def on_device(matrix):
    shape = matrix.shape
    row_blocks, block_size, col_blocks = (shape[0], shape[2], shape[3])
    row_owners = lax.axis_size("row")
    col_owners = lax.axis_size("col")
    row_index = lax.axis_index("row")
    col_index = lax.axis_index("col")
    local_rows = row_blocks * block_size
    trailing = matrix.reshape(local_rows, col_blocks * block_size)
    row_global = jnp.repeat(
        jnp.arange(row_blocks, dtype=jnp.int32) * row_owners + row_index, block_size
    )
    col_global = jnp.arange(col_blocks, dtype=jnp.int32) * col_owners + col_index
    root_col = 0 % col_owners
    local_col = 0 // col_owners
    root_row = 0 % row_owners
    local_row = 0 // row_owners
    column = trailing
    diag_local = column[local_row * block_size : (local_row + 1) * block_size]
    pivot_block = from_root(diag_local, "row", root_row)
    factor = jnp.linalg.cholesky(pivot_block)
    solved = jax.scipy.linalg.solve_triangular(factor, column.T, lower=True).T
    solved = from_root(solved, "col", root_col)
    panel_rows = jnp.where(row_global[:, None] > 0, solved, 0.0)
    pieces = jnp.stack(
        [
            lax.dynamic_slice_in_dim(
                panel_rows, col_global[0] // row_owners * block_size, block_size, 0
            )
        ]
    )
    gathered = lax.all_gather(pieces, "row", axis=0, tiled=True)
    gathered = gathered.reshape(row_owners, col_blocks, block_size, block_size)
    owners = jnp.arange(row_owners, dtype=jnp.int32)
    select = (owners == col_global[0] % row_owners).astype(jnp.float32)
    picks = jnp.sum(select[:, None, None] * gathered[:, 0], axis=0)
    update = lax.dot_general(
        panel_rows,
        picks,
        (((1,), (1,)), ((), ())),
        precision=lax.Precision.HIGHEST,
        preferred_element_type=jnp.float32,
    )
    trailing = trailing - update
    diag_rows = jnp.tile(factor, (row_blocks, 1))
    new_column = jnp.where(
        row_global[:, None] > 0, solved, jnp.where(row_global[:, None] == 0, diag_rows, 0.0)
    )
    old_column = trailing
    is_owner = col_index == root_col
    trailing = trailing.at[:, local_col * block_size : (local_col + 1) * block_size].set(
        jnp.where(is_owner, new_column, old_column)
    )
    return trailing.reshape(shape)


def solution(mesh):
    placed = (P(None, "row", None, None, "col", None),)
    return jax.shard_map(
        on_device,
        mesh=mesh,
        in_specs=placed,
        out_specs=P(None, "row", None, None, "col", None),
        check_vma=False,
    )
```

profile of v0, /device:TPU:3, one launch (start us, length us, event | category | flops | bytes accessed | tf_op | source)
XLA Modules:
  0.0 1384.2 jit_solution(7188762953646616832)
XLA Ops:
  6.5 0.0 all-reduce.3.cloned.1.call-start
  6.5 0.8 slice.30
  7.4 0.1 copy.17
  7.5 0.6 select_bitcast_fusion.1
  8.1 0.0 all-reduce.3.cloned.1.call-update
  8.1 0.0 all-reduce.5.cloned.1.call-start
  8.2 35.5 %all-reduce.3.cloned.1.call-done = f32[128,128]{0,1:T(8,128)} async-done(((f32[128,128]{0,1:T(8,128)}), f32[128,128]{0,1:T(8,128)}) %all-reduce.3.cloned.1.call-update) | async-done | bytes 65552 | tf_op jit(solution)/shard_map/psum | solution.py:9
  43.7 0.9 copy.9
  44.7 0.9 fusion.4
  45.5 11.7 cholesky.15
  57.3 0.6 compare_reduce_fusion
  57.9 0.7 select_bitcast_fusion
  58.6 9.8 custom-call.7
  68.4 8.0 fusion.1
  76.4 0.0 all-reduce.5.cloned.1.call-update
  76.4 5.6 copy.15
  82.0 0.1 broadcast_bitcast_fusion.1
  82.1 0.1 broadcast_bitcast_fusion
  82.2 0.1 copy.11
  82.3 1268.9 %all-reduce.5.cloned.1.call-done = f32[8192,128]{0,1:T(8,128)} async-done(((f32[8192,128]{0,1:T(8,128)}), f32[8192,128]{0,1:T(8,128)}) %all-reduce.5.cloned.1.call-update) | async-done | bytes 4194320 | tf_op jit(solution)/shard_map/psum | solution.py:9
  1351.2 2.5 broadcast_select_fusion
  1353.8 4.0 all-gather
  1357.8 0.1 reshape.75
  1357.9 0.0 copy-start
  1357.9 0.2 multiply_reduce_fusion
  1358.1 0.3 tile.4
  1358.4 1.7 copy-done
  1360.0 11.7 fusion
  1371.8 5.6 copy.16
  (5 shorter events, 0.1 us)
Async XLA Ops:
  6.5 37.2 %all-reduce.3.cloned.1.call-start = ((), (), s32[]{:S(2)}) async-start(), calls=%async_computation | async-start | bytes 131072 | tf_op jit(solution)/shard_map/psum | solution.py:9
  8.1 1343.1 %all-reduce.5.cloned.1.call-start = ((), (), s32[]{:S(2)}) async-start(), calls=%async_computation.1 | async-start | bytes 8388608 | tf_op jit(solution)/shard_map/psum | solution.py:9
  1357.9 2.2 copy-start
Sparse Core Ops, SparseCore 0:
  9.9 33.7 all-reduce.2
  76.5 1274.6 all-reduce.4
where the time goes:
time: 1390 us; the launch traced here: 1380 us
  waiting for transfers between devices  1300 us (94%)
  other arithmetic  27.1 us (2%)
  matrix products  19.7 us (1%)
  local copies, waits for them, and re-layouts  15.3 us (1%)
    psum x2, waiting for transfers between devices, from_root(): return lax.psum(jnp.where(mine, x, jnp.zeros_like(x)), axis)  1300 us
  transfers between devices with their start and end apart: 2, of which 2 were waited for; matrix products, arithmetic and copies ran while one was open for 0% of the time, Pallas kernels for 0%

commit v1 on v0

v1 whole, which is shorter than its diff:
```python
import functools

import jax
import jax.numpy as jnp
from jax import lax
from jax.experimental import pallas as pl
from jax.experimental.pallas import tpu as pltpu
from jax.sharding import PartitionSpec as P

F32 = jnp.float32
BF16 = jnp.bfloat16
NB = 128
HALF = NB // 2
BLOCKS = 64
NX, NY, NZ = 2, 4, 8
NXY = NX * NY
PIVOTS = 16


def split3(x):
    first = x.astype(BF16)
    rest = x - first.astype(F32)
    second = rest.astype(BF16)
    return first, second, (rest - second.astype(F32)).astype(BF16)


def outer(u, t):
    u1, u2, u3 = split3(u)
    t1, t2, t3 = split3(t)
    left = jnp.concatenate([u1, u1, u2, u2, u1, u3], 0)
    right = jnp.concatenate([t1, t2, t1, t2, t3, t1], 0)
    return lax.dot_general(left, right, (((0,), (0,)), ((), ())), preferred_element_type=F32)


def sweep_block(m_ref, ft_ref, block):
    b = PIVOTS
    groups = b // 8
    o = block * b
    sub = lax.broadcasted_iota(jnp.int32, (8, NB), 0)
    lane = lax.broadcasted_iota(jnp.int32, (8, NB), 1)
    rows = [m_ref[o + 8 * t : o + 8 * t + 8, :] for t in range(groups)]
    work = list(rows)
    cols = [[jnp.broadcast_to(rows[t][:, o + j : o + j + 1], (8, NB)) for t in range(groups)] for j in range(b)]
    factor = [None] * groups
    for j in range(b):
        tj, sj = divmod(j, 8)
        pivot = cols[j][tj][sj : sj + 1, :]
        inverse = 1.0 / pivot
        line = work[tj][sj : sj + 1, :] * lax.rsqrt(pivot)
        factor[tj] = jnp.broadcast_to(line, (8, NB)) if sj == 0 else jnp.where(sub == sj, line, factor[tj])
        work = [
            jnp.where(lane == o + j, jnp.where(sub == sj, 1.0, 0.0) if t == tj else 0.0, work[t])
            for t in range(groups)
        ]
        by = list(cols[j])
        by[tj] = jnp.where(sub == sj, cols[j][tj] - 1.0, cols[j][tj])
        scaled = work[tj][sj : sj + 1, :] * inverse
        work = [work[t] - by[t] * scaled for t in range(groups)]
        for m in range(j + 1, b):
            one = cols[m][tj][sj : sj + 1, :] * inverse
            cols[m] = [cols[m][t] - by[t] * one for t in range(groups)]
    inside = (lane >= o) & (lane < o + b)
    eye = [jnp.where(lane == o + 8 * t + sub, 1.0, 0.0) for t in range(groups)]
    left = jnp.concatenate([rows[t] - eye[t] for t in range(groups)], 0)
    right = jnp.concatenate([jnp.where(inside, eye[t] - work[t], work[t]) for t in range(groups)], 0)
    m_ref[...] = m_ref[...] - outer(left, right)
    for t in range(groups):
        s = slice(o + 8 * t, o + 8 * t + 8)
        m_ref[s, :] = jnp.where(inside, -work[t], work[t])
        ft_ref[s, :] = jnp.where(lane >= o + 8 * t + sub, factor[t], 0.0)


def gather_kernel(
    mat_ref, panel, v_ref, ft, pc, pt, a00, s1, s2, sd, sp, sa, sb, rh, ro, ra, rp, lsem
):
    row = lax.axis_index("row")
    col = lax.axis_index("col")
    core = col % 2
    z = (col // 2) % NZ
    y = (col // 16) % NY
    x = col // 64
    mine = col // 2

    def block(bx, by, bz):
        return (bx * NY + by) * NZ + bz

    def device(r, bx, by, bz, k):
        return {"row": r, "col": block(bx, by, bz) * 2 + k}

    def shifted(q):
        return (x + q // NY) % NX, (y + q) % NY

    def push(src, dst, send, recv, to):
        return pltpu.make_async_remote_copy(
            src_ref=src, dst_ref=dst, send_sem=send, recv_sem=recv,
            device_id=to, device_id_type=pl.DeviceIdType.MESH,
        )

    own_half = pl.ds(core * HALF, HALF)
    h0, h1 = pl.ds(0, HALF), pl.ds(HALF, HALF)

    load = pltpu.make_async_copy(mat_ref.at[pl.ds(0, NB)], pc, lsem)

    @pl.when(row == 0)
    def _():
        load.start()

    barrier = pltpu.get_barrier_semaphore()

    def greet(to):
        pl.semaphore_signal(barrier, inc=1, device_id=to, device_id_type=pl.DeviceIdType.MESH)

    for d in range(1, NZ):
        greet(device(row, x, y, (z + d) % NZ, core))
    for q in range(NXY):
        qx, qy = shifted(q)
        if q:
            greet(device(row, qx, qy, z, core))
        greet(device(row, qx, qy, z, 1 - core))
        greet(device(1 - row, qx, qy, z, 1))
        greet(device(1 - row, qx, qy, z, 0))
    for d in range(1, NZ):
        greet(device(1 - row, x, y, (z + d) % NZ, 0))
        greet(device(1 - row, x, y, (z + d) % NZ, 1))
    expected = (NZ - 1) + (NXY - 1) + NXY + 2 * NXY + 2 * (NZ - 1)

    @pl.when(row == 0)
    def _():
        load.wait()
        pt[...] = pc[...].T

        @pl.when(core == 0)
        def _():
            panel[pl.ds(mine, 1), 0:HALF, :] = pt[0:HALF, :][None]

        @pl.when(col == 0)
        def _():
            a00[...] = pc[...]

    pl.semaphore_wait(barrier, expected)

    root = (row == 0) & (col == 0)

    def a00_h0(r, d):
        return push(a00.at[h0], a00.at[h0], sa.at[r * NZ + d], ra.at[0], device(r, 0, 0, d, 0))

    def a00_h1(r, q):
        return push(a00.at[h1], a00.at[h1], sa.at[16 + r * NXY + q], ra.at[1], device(r, q // NY, q % NY, 0, 1))

    def root_sends(act):
        for r in range(2):
            for d in range(NZ):
                if r or d:
                    act(a00_h0(r, d))
            for q in range(NXY):
                act(a00_h1(r, q))

    @pl.when(root)
    def _():
        root_sends(lambda c: c.start())

    def first_h0(d):
        return push(
            pt.at[h0], panel.at[mine, h0], s1.at[d], rh.at[mine], device(core, x, y, (z + d) % NZ, 0)
        )

    def first_h1(q):
        qx, qy = shifted(q)
        return push(pt.at[h1], panel.at[mine, h1], s1.at[NZ + q], rh.at[mine], device(core, qx, qy, z, 1))

    def pivot_rows():
        return push(pc, pc, sp.at[0], rp.at[0], device(1, x, y, z, core))

    def first_sends(act):
        for d in range(NZ):
            if d:
                act(first_h0(d))
            else:

                @pl.when(core == 1)
                def _():
                    act(first_h0(0))

            act(first_h1(d))
        act(pivot_rows())

    @pl.when(row == 0)
    def _():
        first_sends(lambda c: c.start())

    def across(i, half):
        return push(panel.at[i, half], panel.at[i, half], sd.at[i], ro.at[i], device(row, x, y, z, 1 - core))

    def arrived(i, half):
        push(panel.at[i, half], panel.at[i, half], sd.at[i], rh.at[i], device(row, x, y, z, 1 - core)).wait_recv()

    def step(t):
        return jnp.where(t % 2 == 1, (t + 1) // 2, NZ - t // 2)

    def a00_on0(q):
        qx, qy = q // NY, q % NY
        return push(a00.at[h0], a00.at[h0], sb.at[q], ra.at[0], device(row, qx, qy, z, 0))

    def a00_on1(d):
        return push(a00.at[h1], a00.at[h1], sb.at[d], ra.at[1], device(row, x, y, d, 1))

    def a00_across(half, k):
        return push(a00.at[half], a00.at[half], sb.at[8], ra.at[k], device(row, x, y, z, 1 - core))

    def second0(i, t, q):
        qx, qy = shifted(q)
        return push(panel.at[i, h0], panel.at[i, h0], s2.at[t * NXY + q], rh.at[i], device(row, qx, qy, z, 0))

    @pl.when(core == 0)
    def _():
        @pl.when(jnp.logical_not(root))
        def _():
            push(a00.at[h0], a00.at[h0], sb.at[8], ra.at[0], device(row, x, y, z, 1)).wait_recv()

        @pl.when((x == 0) & (y == 0))
        def _():
            for q in range(1, NXY):
                a00_on0(q).start()

        a00_across(h0, 0).start()

        @pl.loop(0, NZ)
        def _(t):
            i = block(x, y, (z + step(t)) % NZ)

            @pl.when((row == 1) | (t > 0))
            def _():
                arrived(i, h0)

            for q in range(1, NXY):
                second0(i, t, q).start()
            across(i, h0).start()

        @pl.loop(0, NZ)
        def _(t):
            for q in range(1, NXY):
                qx, qy = shifted(q)
                i = block(qx, qy, (z + step(t)) % NZ)
                arrived(i, h0)
                across(i, h0).start()

    def second1(i, s, q, way):
        to = device(row, x, y, (z + (1 if way == 0 else NZ - 1)) % NZ, 1)
        return push(panel.at[i, h1], panel.at[i, h1], s2.at[(s * 2 + way) * NXY + q], rh.at[i], to)

    @pl.when(core == 1)
    def _():
        @pl.loop(0, NXY)
        def _(q):
            qx, qy = shifted(q)
            i = block(qx, qy, z)
            arrived(i, h1)
            for way in range(2):
                second1(i, 0, q, way).start()
            across(i, h1).start()

        push(a00.at[h1], a00.at[h1], sb.at[8], ra.at[1], device(row, x, y, z, 0)).wait_recv()

        @pl.when(z == 0)
        def _():
            for d in range(1, NZ):
                a00_on1(d).start()

        @pl.when((row == 1) | (col != 1))
        def _():
            a00_across(h1, 1).start()

        for s in range(1, 4):

            @pl.loop(0, NXY)
            def _(q):
                qx, qy = shifted(q)
                for way in range(2):
                    i = block(qx, qy, (z + (NZ - s if way == 0 else s)) % NZ)
                    arrived(i, h1)
                    if s < 3:
                        second1(i, s, q, way).start()
                    else:

                        @pl.when((qx + qy) % 2 == way)
                        def _():
                            second1(i, s, q, way).start()

                    across(i, h1).start()

        @pl.loop(0, NXY)
        def _(q):
            qx, qy = shifted(q)
            i = block(qx, qy, (z + 4) % NZ)
            arrived(i, h1)
            across(i, h1).start()

    @pl.when((core == 0) & jnp.logical_not(root))
    def _():
        push(a00.at[h1], a00.at[h1], sb.at[8], ra.at[1], device(row, x, y, z, 1)).wait_recv()

    @pl.when(core == 1)
    def _():
        push(a00.at[h0], a00.at[h0], sb.at[8], ra.at[0], device(row, x, y, z, 0)).wait_recv()

    @pl.when(row == 1)
    def _():
        push(pc, pc, sp.at[0], rp.at[0], device(0, x, y, z, core)).wait_recv()

    v_ref[...] = a00[...]
    for k in range(NB // PIVOTS):
        sweep_block(v_ref, ft, k)
    minus_inverse = v_ref[...]
    first = jnp.broadcast_to(col, (NB, NB)) == 0
    rhs = jnp.where(first, -ft[...].T, pc[...])
    v_ref[...] = jnp.dot(minus_inverse, rhs, precision=lax.Precision.HIGHEST, preferred_element_type=F32)

    @pl.loop(0, BLOCKS)
    def _(i):
        other = pl.ds((1 - core) * HALF, HALF)
        push(panel.at[i, other], panel.at[i, other], sd.at[i], ro.at[i], device(row, x, y, z, 1 - core)).wait_recv()

    @pl.loop(0, BLOCKS)
    def _(i):
        across(i, own_half).wait_send()

    @pl.when(root)
    def _():
        root_sends(lambda c: c.wait_send())

    @pl.when(row == 0)
    def _():
        first_sends(lambda c: c.wait_send())

    @pl.when(core == 0)
    def _():
        @pl.when((x == 0) & (y == 0))
        def _():
            for q in range(1, NXY):
                a00_on0(q).wait_send()

        a00_across(h0, 0).wait_send()

        @pl.loop(0, NZ)
        def _(t):
            i = block(x, y, (z + step(t)) % NZ)
            for q in range(1, NXY):
                second0(i, t, q).wait_send()

    @pl.when(core == 1)
    def _():
        @pl.when(z == 0)
        def _():
            for d in range(1, NZ):
                a00_on1(d).wait_send()

        @pl.when((row == 1) | (col != 1))
        def _():
            a00_across(h1, 1).wait_send()

        for s in range(4):

            @pl.loop(0, NXY)
            def _(q):
                qx, qy = shifted(q)
                for way in range(2):
                    i = block(qx, qy, (z + (NZ - s if way == 0 else s)) % NZ)
                    if s < 3:
                        second1(i, s, q, way).wait_send()
                    else:

                        @pl.when((qx + qy) % 2 == way)
                        def _():
                            second1(i, s, q, way).wait_send()


def update_kernel(chunk, panel_ref, mat_ref, v_ref, ft_ref, out_ref):
    first = lax.axis_index("col") == 0
    keep = jnp.where(first, 0.0, 1.0)
    rows = panel_ref[...].reshape(chunk * NB, NB)
    moved = jnp.dot(rows, v_ref[...], precision=lax.Precision.HIGHEST, preferred_element_type=F32)
    out_ref[...] = mat_ref[...] * keep + moved

    @pl.when((pl.program_id(0) == 0) & (lax.axis_index("row") == 0))
    def _():
        out_ref[0:NB, :] = jnp.where(jnp.broadcast_to(lax.axis_index("col"), (NB, NB)) == 0, ft_ref[...].T, mat_ref[0:NB, :])


def on_device(matrix):
    shape = matrix.shape
    local = matrix.reshape(BLOCKS * NB, NB)
    whole = pl.BlockSpec(memory_space=pltpu.VMEM)
    dma = pltpu.SemaphoreType.DMA
    panel, v, ft = pl.pallas_call(
        gather_kernel,
        out_shape=[
            jax.ShapeDtypeStruct((BLOCKS, NB, NB), F32),
            jax.ShapeDtypeStruct((NB, NB), F32),
            jax.ShapeDtypeStruct((NB, NB), F32),
        ],
        in_specs=[pl.BlockSpec(memory_space=pltpu.HBM)],
        out_specs=[whole, whole, whole],
        scratch_shapes=[pltpu.VMEM((NB, NB), F32)] * 3
        + [dma((16,)), dma((64,)), dma((64,)), dma((1,)), dma((32,)), dma((9,))]
        + [dma((64,)), dma((64,)), dma((2,)), dma((1,)), dma],
        compiler_params=pltpu.CompilerParams(
            collective_id=0, has_side_effects=True, vmem_limit_bytes=24 << 20
        ),
        name="gather",
    )(local)
    chunk = 4
    out = pl.pallas_call(
        functools.partial(update_kernel, chunk),
        grid=(BLOCKS // chunk,),
        out_shape=jax.ShapeDtypeStruct((BLOCKS * NB, NB), F32),
        in_specs=[
            pl.BlockSpec((chunk, NB, NB), lambda i: (i, 0, 0)),
            pl.BlockSpec((chunk * NB, NB), lambda i: (i, 0)),
            pl.BlockSpec((NB, NB), lambda i: (0, 0)),
            pl.BlockSpec((NB, NB), lambda i: (0, 0)),
        ],
        out_specs=pl.BlockSpec((chunk * NB, NB), lambda i: (i, 0)),
        name="update",
    )(panel, local, v, ft)
    return out.reshape(shape)


def solution(mesh):
    spec = P(None, "row", None, None, "col", None)
    return jax.shard_map(on_device, mesh=mesh, in_specs=(spec,), out_specs=spec, check_vma=False)
```

time: 1390 us -> 64.8 us (0.05)
  the two profiles are of different devices: /device:TPU:3 before, /device:TPU:8 now
where the time goes in v1:
time: 64.8 us; the launch traced here: 64.3 us
  Pallas kernels  59 us (91%)
  local copies, waits for them, and re-layouts  5.35 us (8%)
    pallas_call x1, Pallas kernels, on_device(): pl.pallas_call(gather_kernel, out_shape=[jax.ShapeDtypeStruct((BLOCKS, NB...  45.4 us
    pallas_call x1, Pallas kernels, on_device(): pl.pallas_call(functools.partial(update_kernel, chunk), grid=(BLOCKS // c...  13.6 us
    unnamed x8, local copies, waits for them, and re-layouts  5.35 us

profile of v1, /device:TPU:8, one launch (start us, length us, event | category | flops | bytes accessed | tf_op | source)
XLA Modules:
  0.0 64.3 jit_solution(8328450461589904838)
XLA Ops:
  0.0 0.0 copy-start
  0.0 2.2 %copy-done = f32[64,1,128,1,1,128]{5,4,3,2,1,0:T(1,128)S(1)} copy-done((f32[64,1,128,1,1,128]{5,4,3,2,1,0:T(1,128)S(1)}, f32[64,1,128,1,1,128]{5,4,3,2,1,0:T(1,128)}, u32[]{:S(2)}) %copy-start) | copy-done | bytes 4194328
  2.2 45.4 %gather.1 = (f32[64,128,128]{2,1,0:T(8,128)S(1)}, f32[128,128]{1,0:T(8,128)S(1)}, f32[128,128]{1,0:T(8,128)S(1)}) custom-call(f32[8192,128]{1,0:T(8,128)S(1)} %bitcast.5), custom_call_target="tpu_custom_call" | custom-call | tf_op jit(solution)/shard_map/gather/pallas_call | solution.py:394
  47.6 0.0 copy-start.1
  47.6 1.9 %copy-done.1 = f32[64,128,128]{2,1,0:T(8,128)} copy-done((f32[64,128,128]{2,1,0:T(8,128)}, f32[64,128,128]{2,1,0:T(8,128)S(1)}, u32[]{:S(2)}) %copy-start.1) | copy-done | bytes 4194328
  49.5 0.0 copy-start.2
  49.5 0.6 copy-done.2
  50.2 0.0 copy-start.3
  50.2 0.6 copy-done.3
  50.8 13.6 %update.1 = f32[8192,128]{1,0:T(8,128)} custom-call(f32[64,128,128]{2,1,0:T(8,128)} %copy-done.1, f32[8192,128]{1,0:T(8,128)} %bitcast.4, f32[128,128]{1,0:T(8,128)} %copy-done.2, f32[128,128]{1,0:T(8,128)} %copy-done.3), custom_call_target="tpu_custom_call" | custom-call | tf_op jit(solution)/shard_map/update/pallas_call | solution.py:412
Async XLA Ops:
  0.0 2.2 %copy-start = (f32[64,1,128,1,1,128]{5,4,3,2,1,0:T(1,128)S(1)}, f32[64,1,128,1,1,128]{5,4,3,2,1,0:T(1,128)}, u32[]{:S(2)}) copy-start(f32[64,1,128,1,1,128]{5,4,3,2,1,0:T(1,128)} %param.1) | copy-start | bytes 12582916
  47.6 1.9 %copy-start.1 = (f32[64,128,128]{2,1,0:T(8,128)}, f32[64,128,128]{2,1,0:T(8,128)S(1)}, u32[]{:S(2)}) copy-start(f32[64,128,128]{2,1,0:T(8,128)S(1)} %get-tuple-element.8.panel_ref) | copy-start | bytes 12582916
  49.5 0.6 copy-start.2
  50.2 0.6 copy-start.3

commit v2 on v0

v2 whole, which is shorter than its diff:
```python
import functools

import jax
import jax.numpy as jnp
from jax import lax
from jax.experimental import pallas as pl
from jax.experimental.pallas import tpu as pltpu
from jax.sharding import PartitionSpec as P

F32 = jnp.float32
BF16 = jnp.bfloat16
NB = 128
HALF = NB // 2
BLOCKS = 64
NX, NY, NZ = 2, 4, 8
NXY = NX * NY
PIVOTS = 16
VMEM_LIMIT = 56 << 20


def split3(x):
    first = x.astype(BF16)
    rest = x - first.astype(F32)
    second = rest.astype(BF16)
    return first, second, (rest - second.astype(F32)).astype(BF16)


def outer(u, t):
    u1, u2, u3 = split3(u)
    t1, t2, t3 = split3(t)
    left = jnp.concatenate([u1, u1, u2, u2, u1, u3], 0)
    right = jnp.concatenate([t1, t2, t1, t2, t3, t1], 0)
    return lax.dot_general(left, right, (((0,), (0,)), ((), ())), preferred_element_type=F32)


def sweep_block(m_ref, ft_ref, block):
    b = PIVOTS
    groups = b // 8
    o = block * b
    sub = lax.broadcasted_iota(jnp.int32, (8, NB), 0)
    lane = lax.broadcasted_iota(jnp.int32, (8, NB), 1)
    rows = [m_ref[o + 8 * t : o + 8 * t + 8, :] for t in range(groups)]
    work = list(rows)
    cols = [[jnp.broadcast_to(rows[t][:, o + j : o + j + 1], (8, NB)) for t in range(groups)] for j in range(b)]
    factor = [None] * groups
    for j in range(b):
        tj, sj = divmod(j, 8)
        pivot = cols[j][tj][sj : sj + 1, :]
        inverse = 1.0 / pivot
        line = work[tj][sj : sj + 1, :] * lax.rsqrt(pivot)
        factor[tj] = jnp.broadcast_to(line, (8, NB)) if sj == 0 else jnp.where(sub == sj, line, factor[tj])
        work = [
            jnp.where(lane == o + j, jnp.where(sub == sj, 1.0, 0.0) if t == tj else 0.0, work[t])
            for t in range(groups)
        ]
        by = list(cols[j])
        by[tj] = jnp.where(sub == sj, cols[j][tj] - 1.0, cols[j][tj])
        scaled = work[tj][sj : sj + 1, :] * inverse
        work = [work[t] - by[t] * scaled for t in range(groups)]
        for m in range(j + 1, b):
            one = cols[m][tj][sj : sj + 1, :] * inverse
            cols[m] = [cols[m][t] - by[t] * one for t in range(groups)]
    inside = (lane >= o) & (lane < o + b)
    eye = [jnp.where(lane == o + 8 * t + sub, 1.0, 0.0) for t in range(groups)]
    left = jnp.concatenate([rows[t] - eye[t] for t in range(groups)], 0)
    right = jnp.concatenate([jnp.where(inside, eye[t] - work[t], work[t]) for t in range(groups)], 0)
    m_ref[...] = m_ref[...] - outer(left, right)
    for t in range(groups):
        s = slice(o + 8 * t, o + 8 * t + 8)
        m_ref[s, :] = jnp.where(inside, -work[t], work[t])
        ft_ref[s, :] = jnp.where(lane >= o + 8 * t + sub, factor[t], 0.0)


def step_kernel(
    mat_ref, out_ref, panel, mine_ref, v_ref, ft, pc, pt, a00, nv, weights,
    s1, sz, s2, sd, sa, sp, r1, r2, ro, ra, rp, lsem
):
    row = lax.axis_index("row")
    col = lax.axis_index("col")
    core = lax.rem(col, 2)
    z = lax.rem(lax.div(col, 2), NZ)
    y = lax.rem(lax.div(col, 2 * NZ), NY)
    x = lax.div(col, 2 * NZ * NY)

    def wrap(v, n):
        return jnp.where(v >= n, v - n, v)

    xs = [x, 1 - x]
    ys = [wrap(y + d, NY) for d in range(NY)]
    zs = [wrap(z + d, NZ) for d in range(NZ)]
    offsets = [(1, 2), (1, 1), (1, 3), (0, 2), (1, 0), (0, 1), (0, 3)]
    line = [0, 1, 7, 2, 6, 3, 5, 4]

    def device(r, bx, by, bz, k):
        return {"row": r, "col": bx * (2 * NZ * NY) + by * (2 * NZ) + bz * 2 + k}

    def at(qx, qy):
        return xs[qx % NX] * NY + ys[qy % NY]

    here = at(0, 0)

    def push(src, dst, send, recv, to):
        return pltpu.make_async_remote_copy(
            src_ref=src, dst_ref=dst, send_sem=send, recv_sem=recv,
            device_id=to, device_id_type=pl.DeviceIdType.MESH,
        )

    sibling = device(row, x, y, z, 1 - core)

    def wait_bytes(ref, sem):
        push(ref, ref, sem, sem, sibling).wait_recv()

    def wait_sent(ref, sem):
        push(ref, ref, sem, sem, sibling).wait_send()

    h0, h1 = pl.ds(0, HALF), pl.ds(HALF, HALF)
    root = (row == 0) & (col == 0)

    load = pltpu.make_async_copy(mat_ref.at[0, 0], pc, lsem.at[0])
    load_all = pltpu.make_async_copy(mat_ref, mine_ref, lsem.at[1])

    @pl.when(row == 0)
    def _():
        load.start()

    load_all.start()

    barrier = pltpu.get_barrier_semaphore()

    def greet(to):
        pl.semaphore_signal(barrier, inc=1, device_id=to, device_id_type=pl.DeviceIdType.MESH)

    greet(sibling)
    greet(device(1 - row, x, y, z, core))
    for d in (1, NZ - 1):
        greet(device(row, x, y, zs[d], core))

    @pl.when(core == 0)
    def _():
        for d in range(2, NZ - 1):
            greet(device(row, x, y, zs[d], 0))
        for qx, qy in offsets:
            greet(device(row, xs[qx], ys[qy], z, 0))

    @pl.when(core == 1)
    def _():
        for qx, qy in offsets:
            greet(device(1 - row, xs[qx], ys[qy], z, 1))

    @pl.when(row == 0)
    def _():
        for qx, qy in offsets:
            greet(device(0, xs[qx], ys[qy], z, 1 - core))

    @pl.when(row != core)
    def _():
        for qx in range(NX):
            greet(device(1 - row, xs[qx], y, z, 1 - core))

    @pl.when(root)
    def _():
        for q in range(1, NXY):
            greet(device(1, q // NY, q % NY, 0, 0))

    @pl.when((row == 1) & (core == 0) & (z == 0) & (here > 0))
    def _():
        greet(device(0, 0, 0, 0, 0))

    heard = 4 + (NZ - 3 + NXY - 1) * (1 - core) + (NXY - 1) * core + (NXY - 1) * (1 - row)
    heard += jnp.where(row != core, NX, 0) + jnp.where(root, NXY - 1, 0)
    heard += jnp.where((row == 1) & (core == 0) & (z == 0) & (here > 0), 1, 0)

    @pl.when(row == 0)
    def _():
        load.wait()
        pt[...] = pc[...].T

        @pl.when(core == 0)
        def _():
            panel[pl.ds(here, 1), pl.ds(z, 1), 0:HALF, :] = pt[0:HALF, :][None, None]

        @pl.when(col == 0)
        def _():
            a00[...] = pc[...]

    pl.semaphore_wait(barrier, heard)

    def a00_push(i, to):
        return push(a00, a00, sa.at[i], ra.at[0], to)

    def root_sends(act):
        for n, d in enumerate([4, 3, 5, 2, 6, 1, 7]):
            act(a00_push(n, device(0, 0, 0, d, 0)))
        for n, q in enumerate([6, 5, 7, 2, 4, 1, 3, 0]):
            act(a00_push(7 + n, device(1, q // NY, q % NY, 0, 0)))

    def second_sends(act):
        @pl.when((row == 0) & (here == 0))
        def _():
            for n, (qx, qy) in enumerate(offsets):
                act(a00_push(15 + n, device(0, qx, qy, z, 0)))

        @pl.when((row == 1) & (z == 0))
        def _():
            for n, d in enumerate([4, 3, 5, 2, 6, 1, 7]):
                act(a00_push(15 + n, device(1, x, y, d, 0)))

    def a00_wait():
        @pl.when(jnp.logical_not(root))
        def _():
            wait_bytes(a00, ra.at[0])

    @pl.when(root)
    def _():
        root_sends(lambda c: c.start())
        second_sends(lambda c: c.start())

    def cross(d, half):
        group = panel.at[:, zs[d], half]
        push(group, group, sd.at[0], ro.at[d], sibling).start()

    def set_weights(rhs, minus_inverse):
        v = jnp.dot(minus_inverse[...], rhs, precision=lax.Precision.HIGHEST, preferred_element_type=F32)
        high = v.astype(BF16)
        low = (v - high.astype(F32)).astype(BF16)
        both = jnp.concatenate([high, low], 1)
        weights[...] = jnp.concatenate([both, both], 0)

    keep = jnp.where(col == 0, 0.0, 1.0)

    def update(d, half):
        there = (slice(None), pl.ds(zs[d], 1), slice(half * HALF, (half + 1) * HALF), slice(None))
        rows = panel[there].reshape(NXY * HALF, NB)
        high = rows.astype(BF16)
        low = (rows - high.astype(F32)).astype(BF16)
        parts = jnp.dot(jnp.concatenate([high, low], 1), weights[...], preferred_element_type=F32)
        moved = (parts[:, :NB] + parts[:, NB:]).reshape(NXY, 1, HALF, NB)
        out_ref[there] = mine_ref[there] * keep + moved

    def along_z(src, q, d):
        return push(src, panel.at[at(q, 0), z, h0], sz.at[0], r1.at[q * NZ + d], device(row, x, y, zs[-d % NZ], 0))

    def first_x(q):
        return push(pt.at[h0], panel.at[here, z, h0], s1.at[0], r1.at[q * NZ], device(core, xs[q], y, z, 0))

    def first_h1(n, qx, qy):
        return push(pt.at[h1], panel.at[here, z, h1], s1.at[0], r1.at[n], device(core, xs[qx], ys[qy], z, 1))

    def pivot_rows():
        return push(pc, pc, sp.at[0], rp.at[0], device(1, x, y, z, core))

    @pl.when(row == 0)
    def _():
        first_x(1).start()

        @pl.when(core == 1)
        def _():
            first_x(0).start()

        first_h1(7, 0, 0).start()
        for n in range(NXY - 1):
            first_h1(n, *offsets[n]).start()

            @pl.when(core == 0)
            def _():
                along_z(pt.at[h0], 0, line[n + 1]).start()

        pivot_rows().start()

    @pl.when(core == 0)
    def _():
        def along_y(q, d):
            piece = panel.at[at(q, 0), zs[d], h0]
            for qy in (2, 1, 3):
                push(piece, piece, s2.at[0], r2.at[d], device(row, x, ys[qy], z, 0)).start()

        def wait_line(q, d):
            wait_bytes(pt.at[h0], r1.at[q * NZ + d])

        def spread(q):
            for d in line[1:]:
                along_z(panel.at[at(q, 0), z, h0], q, d).start()

        @pl.when(row == 1)
        def _():
            wait_line(0, 0)
            spread(0)

        along_y(0, 0)
        wait_line(1, 0)
        spread(1)
        along_y(1, 0)

        def a00_on():
            @pl.when(((row == 0) & (here == 0) & (col > 0)) | ((row == 1) & (z == 0)))
            def _():
                wait_bytes(a00, ra.at[0])
                second_sends(lambda c: c.start())

        for n, d in enumerate(line[1:]):
            wait_line(0, d)
            along_y(0, d)
            if n == 1:
                a00_on()
        for d in line[1:]:
            wait_line(1, d)
            along_y(1, d)
        @pl.when(jnp.logical_not(((row == 0) & (here == 0)) | ((row == 1) & (z == 0))))
        def _():
            wait_bytes(a00, ra.at[0])
        @pl.when(row == 1)
        def _():
            wait_bytes(pc, rp.at[0])

        load_all.wait()
        v_ref[...] = a00[...]
        for n in range(NB // PIVOTS):
            sweep_block(v_ref, ft, n)
        push(v_ref, nv, sp.at[1], rp.at[1], sibling).start()
        first = jnp.broadcast_to(col, (NB, NB)) == 0
        set_weights(jnp.where(first, -ft[...].T, pc[...]), v_ref)

        for n, d in enumerate(line):
            wait_bytes(panel.at[pl.ds(0, NXY - 2), 0, h0], r2.at[d])
            cross(d, h0)
            update(d, 0)

    @pl.when(core == 1)
    def _():
        sources = [(0, 0)] + [(-qx, -qy) for qx, qy in offsets]
        sems = [7, 0, 1, 2, 3, 4, 5, 6]

        def ring(i, s, n, way):
            piece = panel.at[i, zs[-s % NZ] if way == 0 else zs[s], h1]
            to = device(row, x, y, zs[1] if way == 0 else zs[7], 1)
            return push(piece, piece, s2.at[0], r2.at[(s * 2 + way) * NXY + n], to)

        for n, (qx, qy) in enumerate(sources):
            i = at(qx, qy)
            wait_bytes(panel.at[i, z, h1], r1.at[sems[n]])
            for way in range(2):
                ring(i, 0, n, way).start()
        cross(0, h1)
        for s in range(1, 4):
            for n, (qx, qy) in enumerate(sources):
                i = at(qx, qy)
                for way in range(2):
                    wait_bytes(panel.at[i, z, h1], r2.at[((s - 1) * 2 + way) * NXY + n])
                    if s < 3:
                        ring(i, s, n, way).start()
                    elif n % 2 == way:
                        ring(i, s, n, way).start()
            cross(-s % NZ, h1)
            cross(s, h1)
        for n, (qx, qy) in enumerate(sources):
            i = at(qx, qy)
            wait_bytes(panel.at[i, z, h1], r2.at[(3 * 2 + n % 2) * NXY + n])
        cross(4, h1)

        @pl.when(row == 1)
        def _():
            wait_bytes(pc, rp.at[0])
        load_all.wait()
        wait_bytes(nv, rp.at[1])
        set_weights(pc[...], nv)
        for d in line:
            update(d, 1)

    @pl.when(core == 0)
    def _():
        for d in line:
            wait_bytes(panel.at[:, 0, h0], ro.at[d])
            update(d, 1)

    @pl.when(core == 1)
    def _():
        for d in line:
            wait_bytes(panel.at[:, 0, h0], ro.at[d])
            update(d, 0)

    @pl.when(row == 0)
    def _():
        head = mine_ref[0, 0]
        out_ref[0, 0] = jnp.where(jnp.broadcast_to(col, (NB, NB)) == 0, ft[...].T, head)

    wait_sent(panel.at[:, :, h0], sd.at[0])

    @pl.when(core == 0)
    def _():
        wait_sent(v_ref, sp.at[1])

    @pl.when(root)
    def _():
        root_sends(lambda c: c.wait_send())

    @pl.when(core == 0)
    def _():
        second_sends(lambda c: c.wait_send())
    @pl.when(row == 0)
    def _():
        wait_sent(panel.at[0, :, h0], s1.at[0])
        wait_sent(pt.at[h0], s1.at[0])

        @pl.when(core == 1)
        def _():
            wait_sent(pt.at[h0], s1.at[0])

        wait_sent(pc, sp.at[0])

    @pl.when(core == 0)
    def _():
        wait_sent(panel.at[pl.ds(0, 2), pl.ds(0, NZ - 1), h0], sz.at[0])
        wait_sent(panel.at[pl.ds(0, 6), :, h0], s2.at[0])
    @pl.when(core == 1)
    def _():
        wait_sent(panel.at[pl.ds(0, NXY - 1), :, h0], s2.at[0])


def on_device_gather(matrix):
    shape = (NXY, NZ, NB, NB)
    dma = pltpu.SemaphoreType.DMA
    block = pltpu.VMEM((NB, NB), F32)
    return pl.pallas_call(
        step_kernel,
        out_shape=pltpu.VMEM(shape, F32),
        in_specs=[pl.BlockSpec(memory_space=pltpu.HBM)],
        out_specs=pl.BlockSpec(memory_space=pltpu.VMEM),
        scratch_shapes=[pltpu.VMEM(shape, F32)] * 2
        + [block] * 6
        + [pltpu.VMEM((2 * NB, 2 * NB), BF16)]
        + [dma((1,)), dma((1,)), dma((1,)), dma((1,)), dma((22,)), dma((2,))]
        + [dma((16,)), dma((64,)), dma((8,)), dma((1,)), dma((2,)), dma((2,))],
        compiler_params=pltpu.CompilerParams(
            collective_id=0, has_side_effects=True, vmem_limit_bytes=VMEM_LIMIT
        ),
        name="step",
    )(matrix)


def on_device(matrix):
    local = matrix.reshape(NXY, NZ, NB, NB)
    return on_device_gather(local).reshape(matrix.shape)


def solution(mesh):
    spec = P(None, "row", None, None, "col", None)
    return jax.shard_map(on_device, mesh=mesh, in_specs=(spec,), out_specs=spec, check_vma=False)
```

time: 1390 us -> 37.7 us (0.03)
  waiting for transfers between devices: 1300 us -> 0 us
  Pallas kernels: 0 us -> 35.6 us
  other arithmetic: 27.1 us -> 0 us
  matrix products: 19.7 us -> 0 us
    psum x2 -> x0, waiting for transfers between devices: 1300 us -> none  [from_root(): return lax.psum(jnp.where(mine, x, jnp.zeros_like(x)), axis)]
    pallas_call x0 -> x1, Pallas kernels: none -> 35.6 us  [on_device_gather(): pl.pallas_call(step_kernel, out_shape=pltpu.VMEM(shape, F32), in_specs=[p...]
    another operation x5 -> x0, other arithmetic: 22.9 us -> none  [the longest x3 12.4 us: on_device(): factor = jnp.linalg.cholesky(pivot_block)]
  transfers between devices with their start and end apart: 2 -> 0, of which waited for: 2 -> 0; matrix products, arithmetic and copies ran while one was open for 0% -> 0% of each run, Pallas kernels for 0% -> 0%
where the time goes in v2:
time: 37.7 us; the launch traced here: 37.6 us
  Pallas kernels  35.6 us (94%)
  local copies, waits for them, and re-layouts  2.02 us (5%)
    pallas_call x1, Pallas kernels, on_device_gather(): pl.pallas_call(step_kernel, out_shape=pltpu.VMEM(shape, F32), in_specs=[p...  35.6 us
    unnamed x1, local copies, waits for them, and re-layouts  2.02 us

profile of v2, /device:TPU:3, one launch (start us, length us, event | category | flops | bytes accessed | tf_op | source)
XLA Modules:
  0.0 37.6 jit_solution(11643507681571347032)
XLA Ops:
  0.0 35.6 %step.1 = f32[8,8,128,128]{3,2,1,0:T(8,128)S(1)} custom-call(f32[8,8,128,128]{3,2,1,0:T(8,128)} %bitcast.5), custom_call_target="tpu_custom_call" | custom-call | tf_op jit(solution)/shard_map/step/pallas_call | solution.py:423
  35.6 2.0 %copy.4 = f32[64,1,128,1,1,128]{5,4,3,2,1,0:T(1,128)} copy(f32[64,1,128,1,1,128]{5,4,3,2,1,0:T(1,128)S(1)} %bitcast.4) | data formatting | bytes 8388608

commit v3 on v2

--- a/solution.py
+++ b/solution.py
@@ -11,6 +11,7 @@
 BF16 = jnp.bfloat16
 NB = 128
 HALF = NB // 2
+HA = 56
 BLOCKS = 64
 NX, NY, NZ = 2, 4, 8
 NXY = NX * NY
@@ -71,8 +72,30 @@
         ft_ref[s, :] = jnp.where(lane >= o + 8 * t + sub, factor[t], 0.0)
 
 
+def pack(block):
+    sub = lax.broadcasted_iota(jnp.int32, (HALF, NB), 0)
+    lane = lax.broadcasted_iota(jnp.int32, (HALF, NB), 1)
+    top, bottom = block[:HALF], block[HALF:]
+    body = jnp.where(sub > lane, pltpu.roll(bottom, HALF, 1), top)
+    diagonal = jnp.sum(jnp.where(lane == sub + HALF, bottom, 0.0), axis=0, keepdims=True)
+    return jnp.concatenate([body, jnp.broadcast_to(diagonal, (8, NB))], 0)
+
+
+def unpack(ref):
+    sub = lax.broadcasted_iota(jnp.int32, (HALF, NB), 0)
+    lane = lax.broadcasted_iota(jnp.int32, (HALF, NB), 1)
+    body = ref[0:HALF, :]
+    last = pltpu.roll(jnp.where(sub > lane, body, 0.0), HALF, 1)
+    strict = jnp.concatenate([jnp.where(sub < lane, body, 0.0), last], 0)
+    diagonal = jnp.broadcast_to(ref[HALF : HALF + 1, :], (HALF, NB))
+    diagonal = jnp.concatenate(
+        [jnp.where(sub == lane, body, 0.0), jnp.where(lane == sub + HALF, diagonal, 0.0)], 0
+    )
+    return strict + strict.T + diagonal
+
+
 def step_kernel(
-    mat_ref, out_ref, panel, mine_ref, v_ref, ft, pc, pt, a00, nv, weights,
+    mat_ref, out_ref, panel, mine_ref, v_ref, ft, pc, pt, packed, nv, weights,
     s1, sz, s2, sd, sa, sp, r1, r2, ro, ra, rp, lsem
 ):
     row = lax.axis_index("row")
@@ -113,7 +136,7 @@
     def wait_sent(ref, sem):
         push(ref, ref, sem, sem, sibling).wait_send()
 
-    h0, h1 = pl.ds(0, HALF), pl.ds(HALF, HALF)
+    h0, h1 = pl.ds(0, HA), pl.ds(HA, NB - HA)
     root = (row == 0) & (col == 0)
 
     load = pltpu.make_async_copy(mat_ref.at[0, 0], pc, lsem.at[0])
@@ -177,16 +200,16 @@
 
         @pl.when(core == 0)
         def _():
-            panel[pl.ds(here, 1), pl.ds(z, 1), 0:HALF, :] = pt[0:HALF, :][None, None]
+            panel[pl.ds(here, 1), pl.ds(z, 1), 0:HA, :] = pt[0:HA, :][None, None]
 
         @pl.when(col == 0)
         def _():
-            a00[...] = pc[...]
+            packed[...] = pack(pc[...])
 
     pl.semaphore_wait(barrier, heard)
 
     def a00_push(i, to):
-        return push(a00, a00, sa.at[i], ra.at[0], to)
+        return push(packed, packed, sa.at[i], ra.at[0], to)
 
     def root_sends(act):
         for n, d in enumerate([4, 3, 5, 2, 6, 1, 7]):
@@ -204,11 +227,6 @@
         def _():
             for n, d in enumerate([4, 3, 5, 2, 6, 1, 7]):
                 act(a00_push(15 + n, device(1, x, y, d, 0)))
-
-    def a00_wait():
-        @pl.when(jnp.logical_not(root))
-        def _():
-            wait_bytes(a00, ra.at[0])
 
     @pl.when(root)
     def _():
@@ -228,14 +246,20 @@
 
     keep = jnp.where(col == 0, 0.0, 1.0)
 
-    def update(d, half):
-        there = (slice(None), pl.ds(zs[d], 1), slice(half * HALF, (half + 1) * HALF), slice(None))
-        rows = panel[there].reshape(NXY * HALF, NB)
+    def update(d, start, size):
+        there = (slice(None), pl.ds(zs[d], 1), slice(start, start + size), slice(None))
+        rows = panel[there].reshape(NXY * size, NB)
         high = rows.astype(BF16)
         low = (rows - high.astype(F32)).astype(BF16)
         parts = jnp.dot(jnp.concatenate([high, low], 1), weights[...], preferred_element_type=F32)
-        moved = (parts[:, :NB] + parts[:, NB:]).reshape(NXY, 1, HALF, NB)
+        moved = (parts[:, :NB] + parts[:, NB:]).reshape(NXY, 1, size, NB)
         out_ref[there] = mine_ref[there] * keep + moved
+
+    def update0(d):
+        update(d, 0, HA)
+
+    def update1(d):
+        update(d, HA, NB - HA)
 
     def along_z(src, q, d):
         return push(src, panel.at[at(q, 0), z, h0], sz.at[0], r1.at[q * NZ + d], device(row, x, y, zs[-d % NZ], 0))
@@ -244,19 +268,18 @@
         return push(pt.at[h0], panel.at[here, z, h0], s1.at[0], r1.at[q * NZ], device(core, xs[q], y, z, 0))
 
     def first_h1(n, qx, qy):
-        return push(pt.at[h1], panel.at[here, z, h1], s1.at[0], r1.at[n], device(core, xs[qx], ys[qy], z, 1))
+        return push(pt.at[h1], panel.at[here, z, h1], s1.at[1], r1.at[n], device(core, xs[qx], ys[qy], z, 1))
 
     def pivot_rows():
         return push(pc, pc, sp.at[0], rp.at[0], device(1, x, y, z, core))
 
     @pl.when(row == 0)
     def _():
+        @pl.when(core == 1)
+        def _():
+            first_x(0).start()
+
         first_x(1).start()
-
-        @pl.when(core == 1)
-        def _():
-            first_x(0).start()
-
         first_h1(7, 0, 0).start()
         for n in range(NXY - 1):
             first_h1(n, *offsets[n]).start()
@@ -264,8 +287,6 @@
             @pl.when(core == 0)
             def _():
                 along_z(pt.at[h0], 0, line[n + 1]).start()
-
-        pivot_rows().start()
 
     @pl.when(core == 0)
     def _():
@@ -294,7 +315,7 @@
         def a00_on():
             @pl.when(((row == 0) & (here == 0) & (col > 0)) | ((row == 1) & (z == 0)))
             def _():
-                wait_bytes(a00, ra.at[0])
+                wait_bytes(packed, ra.at[0])
                 second_sends(lambda c: c.start())
 
         for n, d in enumerate(line[1:]):
@@ -302,28 +323,51 @@
             along_y(0, d)
             if n == 1:
                 a00_on()
+
+        @pl.when(row == 0)
+        def _():
+            pivot_rows().start()
+
         for d in line[1:]:
             wait_line(1, d)
             along_y(1, d)
+
         @pl.when(jnp.logical_not(((row == 0) & (here == 0)) | ((row == 1) & (z == 0))))
         def _():
-            wait_bytes(a00, ra.at[0])
-        @pl.when(row == 1)
-        def _():
-            wait_bytes(pc, rp.at[0])
-
-        load_all.wait()
-        v_ref[...] = a00[...]
+            wait_bytes(packed, ra.at[0])
+        def group(n):
+            wait_bytes(panel.at[pl.ds(0, NXY - 2), 0, h0], r2.at[line[n]])
+            cross(line[n], h0)
+
+        def other(d):
+            wait_bytes(panel.at[:, 0, h1], ro.at[d])
+            update1(d)
+
+        v_ref[...] = unpack(packed)
+        done = 0
         for n in range(NB // PIVOTS):
             sweep_block(v_ref, ft, n)
+            if n >= 3:
+                group(done)
+                done += 1
         push(v_ref, nv, sp.at[1], rp.at[1], sibling).start()
+
+        @pl.when(row == 1)
+        def _():
+            wait_bytes(pc, rp.at[0])
+
         first = jnp.broadcast_to(col, (NB, NB)) == 0
         set_weights(jnp.where(first, -ft[...].T, pc[...]), v_ref)
-
-        for n, d in enumerate(line):
-            wait_bytes(panel.at[pl.ds(0, NXY - 2), 0, h0], r2.at[d])
-            cross(d, h0)
-            update(d, 0)
+        load_all.wait()
+        for n in range(done):
+            update0(line[n])
+        for d in line[:3]:
+            other(d)
+        for n in range(done, NZ):
+            group(n)
+            update0(line[n])
+        for d in line[3:]:
+            other(d)
 
     @pl.when(core == 1)
     def _():
@@ -341,6 +385,11 @@
             for way in range(2):
                 ring(i, 0, n, way).start()
         cross(0, h1)
+
+        @pl.when(row == 0)
+        def _():
+            pivot_rows().start()
+
         for s in range(1, 4):
             for n, (qx, qy) in enumerate(sources):
                 i = at(qx, qy)
@@ -352,38 +401,35 @@
                         ring(i, s, n, way).start()
             cross(-s % NZ, h1)
             cross(s, h1)
+        @pl.when(row == 1)
+        def _():
+            wait_bytes(pc, rp.at[0])
+
+        def other(d):
+            wait_bytes(panel.at[:, 0, h0], ro.at[d])
+            update0(d)
+
+        load_all.wait()
+        wait_bytes(nv, rp.at[1])
+        set_weights(pc[...], nv)
+        for d in line[:5]:
+            update1(d)
+        for d in line[:4]:
+            other(d)
         for n, (qx, qy) in enumerate(sources):
             i = at(qx, qy)
             wait_bytes(panel.at[i, z, h1], r2.at[(3 * 2 + n % 2) * NXY + n])
         cross(4, h1)
-
-        @pl.when(row == 1)
-        def _():
-            wait_bytes(pc, rp.at[0])
-        load_all.wait()
-        wait_bytes(nv, rp.at[1])
-        set_weights(pc[...], nv)
-        for d in line:
-            update(d, 1)
-
-    @pl.when(core == 0)
-    def _():
-        for d in line:
-            wait_bytes(panel.at[:, 0, h0], ro.at[d])
-            update(d, 1)
-
-    @pl.when(core == 1)
-    def _():
-        for d in line:
-            wait_bytes(panel.at[:, 0, h0], ro.at[d])
-            update(d, 0)
+        for d in line[5:]:
+            update1(d)
+        for d in line[4:]:
+            other(d)
 
     @pl.when(row == 0)
     def _():
         head = mine_ref[0, 0]
         out_ref[0, 0] = jnp.where(jnp.broadcast_to(col, (NB, NB)) == 0, ft[...].T, head)
 
-    wait_sent(panel.at[:, :, h0], sd.at[0])
 
     @pl.when(core == 0)
     def _():
@@ -398,7 +444,7 @@
         second_sends(lambda c: c.wait_send())
     @pl.when(row == 0)
     def _():
-        wait_sent(panel.at[0, :, h0], s1.at[0])
+        wait_sent(panel.at[0, :, h1], s1.at[1])
         wait_sent(pt.at[h0], s1.at[0])
 
         @pl.when(core == 1)
@@ -409,11 +455,13 @@
 
     @pl.when(core == 0)
     def _():
+        wait_sent(panel.at[:, :, h0], sd.at[0])
         wait_sent(panel.at[pl.ds(0, 2), pl.ds(0, NZ - 1), h0], sz.at[0])
         wait_sent(panel.at[pl.ds(0, 6), :, h0], s2.at[0])
     @pl.when(core == 1)
     def _():
-        wait_sent(panel.at[pl.ds(0, NXY - 1), :, h0], s2.at[0])
+        wait_sent(panel.at[:, :, h1], sd.at[0])
+        wait_sent(panel.at[pl.ds(0, NXY - 1), :, h1], s2.at[0])
 
 
 def on_device_gather(matrix):
@@ -426,9 +474,9 @@
         in_specs=[pl.BlockSpec(memory_space=pltpu.HBM)],
         out_specs=pl.BlockSpec(memory_space=pltpu.VMEM),
         scratch_shapes=[pltpu.VMEM(shape, F32)] * 2
-        + [block] * 6
-        + [pltpu.VMEM((2 * NB, 2 * NB), BF16)]
-        + [dma((1,)), dma((1,)), dma((1,)), dma((1,)), dma((22,)), dma((2,))]
+        + [block] * 4
+        + [pltpu.VMEM((HALF + 8, NB), F32), block, pltpu.VMEM((2 * NB, 2 * NB), BF16)]
+        + [dma((2,)), dma((1,)), dma((1,)), dma((1,)), dma((22,)), dma((2,))]
         + [dma((16,)), dma((64,)), dma((8,)), dma((1,)), dma((2,)), dma((2,))],
         compiler_params=pltpu.CompilerParams(
             collective_id=0, has_side_effects=True, vmem_limit_bytes=VMEM_LIMIT

time: 37.7 us -> 36.2 us (0.960)
  Pallas kernels: 35.6 us -> 34.1 us
    pallas_call x1, Pallas kernels: 35.6 us -> 34.1 us  [on_device_gather(): pl.pallas_call(step_kernel, out_shape=pltpu.VMEM(shape, F32), in_specs=[p...]
where the time goes in v3:
time: 36.2 us; the launch traced here: 36.1 us
  Pallas kernels  34.1 us (94%)
  local copies, waits for them, and re-layouts  2.02 us (6%)
    pallas_call x1, Pallas kernels, on_device_gather(): pl.pallas_call(step_kernel, out_shape=pltpu.VMEM(shape, F32), in_specs=[p...  34.1 us
    unnamed x1, local copies, waits for them, and re-layouts  2.02 us

profile of v3, /device:TPU:3, one launch (start us, length us, event | category | flops | bytes accessed | tf_op | source)
XLA Modules:
  0.0 36.1 jit_solution(14700439359470055402)
XLA Ops:
  0.0 34.1 %step.1 = f32[8,8,128,128]{3,2,1,0:T(8,128)S(1)} custom-call(f32[8,8,128,128]{3,2,1,0:T(8,128)} %bitcast.5), custom_call_target="tpu_custom_call" | custom-call | tf_op jit(solution)/shard_map/step/pallas_call | solution.py:471
  34.1 2.0 %copy.4 = f32[64,1,128,1,1,128]{5,4,3,2,1,0:T(1,128)} copy(f32[64,1,128,1,1,128]{5,4,3,2,1,0:T(1,128)S(1)} %bitcast.4) | data formatting | bytes 8388608

commit v4 on v3

--- a/solution.py
+++ b/solution.py
@@ -359,15 +359,13 @@
         first = jnp.broadcast_to(col, (NB, NB)) == 0
         set_weights(jnp.where(first, -ft[...].T, pc[...]), v_ref)
         load_all.wait()
-        for n in range(done):
-            update0(line[n])
-        for d in line[:3]:
-            other(d)
-        for n in range(done, NZ):
-            group(n)
-            update0(line[n])
-        for d in line[3:]:
-            other(d)
+        for n, (before, theirs) in enumerate([((0, 1), (0,)), ((2, 3), (1, 7)), ((4, 5), (2, 6)), ((6, 7), (3, 5, 4))]):
+            for m in before:
+                update0(line[m])
+            for d in theirs:
+                other(d)
+            if n < NZ - done:
+                group(done + n)
 
     @pl.when(core == 1)
     def _():
@@ -419,7 +417,8 @@
         for n, (qx, qy) in enumerate(sources):
             i = at(qx, qy)
             wait_bytes(panel.at[i, z, h1], r2.at[(3 * 2 + n % 2) * NXY + n])
-        cross(4, h1)
+            piece = panel.at[i, zs[4], h1]
+            push(piece, piece, sd.at[0], ro.at[4], sibling).start()
         for d in line[5:]:
             update1(d)
         for d in line[4:]:

time: 36.2 us -> 36.2 us (level)
  no operation moved by 1% of the time
where the time goes in v4:
time: 36.2 us; the launch traced here: 36.1 us
  Pallas kernels  34.1 us (94%)
  local copies, waits for them, and re-layouts  2.02 us (6%)
    pallas_call x1, Pallas kernels, on_device_gather(): pl.pallas_call(step_kernel, out_shape=pltpu.VMEM(shape, F32), in_specs=[p...  34.1 us
    unnamed x1, local copies, waits for them, and re-layouts  2.02 us

profile of v4, /device:TPU:3, one launch (start us, length us, event | category | flops | bytes accessed | tf_op | source)
XLA Modules:
  0.0 36.1 jit_solution(14965090886719812082)
XLA Ops:
  0.0 34.1 %step.1 = f32[8,8,128,128]{3,2,1,0:T(8,128)S(1)} custom-call(f32[8,8,128,128]{3,2,1,0:T(8,128)} %bitcast.5), custom_call_target="tpu_custom_call" | custom-call | tf_op jit(solution)/shard_map/step/pallas_call | solution.py:470
  34.1 2.0 %copy.4 = f32[64,1,128,1,1,128]{5,4,3,2,1,0:T(1,128)} copy(f32[64,1,128,1,1,128]{5,4,3,2,1,0:T(1,128)S(1)} %bitcast.4) | data formatting | bytes 8388608

commit v5 on v4

--- a/solution.py
+++ b/solution.py
@@ -146,7 +146,6 @@
     def _():
         load.start()
 
-    load_all.start()
 
     barrier = pltpu.get_barrier_semaphore()
 
@@ -287,6 +286,8 @@
             @pl.when(core == 0)
             def _():
                 along_z(pt.at[h0], 0, line[n + 1]).start()
+
+    load_all.start()
 
     @pl.when(core == 0)
     def _():

time: 36.2 us -> 36.2 us (level)
  no operation moved by 1% of the time
where the time goes in v5:
time: 36.2 us; the launch traced here: 36.1 us
  Pallas kernels  34.1 us (94%)
  local copies, waits for them, and re-layouts  2.02 us (6%)
    pallas_call x1, Pallas kernels, on_device_gather(): pl.pallas_call(step_kernel, out_shape=pltpu.VMEM(shape, F32), in_specs=[p...  34.1 us
    unnamed x1, local copies, waits for them, and re-layouts  2.02 us

profile of v5, /device:TPU:3, one launch (start us, length us, event | category | flops | bytes accessed | tf_op | source)
XLA Modules:
  0.0 36.1 jit_solution(15783630261938564231)
XLA Ops:
  0.0 34.1 %step.1 = f32[8,8,128,128]{3,2,1,0:T(8,128)S(1)} custom-call(f32[8,8,128,128]{3,2,1,0:T(8,128)} %bitcast.5), custom_call_target="tpu_custom_call" | custom-call | tf_op jit(solution)/shard_map/step/pallas_call | solution.py:471
  34.1 2.0 %copy.4 = f32[64,1,128,1,1,128]{5,4,3,2,1,0:T(1,128)} copy(f32[64,1,128,1,1,128]{5,4,3,2,1,0:T(1,128)S(1)} %bitcast.4) | data formatting | bytes 8388608
